TPU v7x, 512 devices: a whole 4x4x16 slice. The times are simulated.
512 devices in a mesh: seq: 128 (over z_hi, x, y, core), head: 4 (over z_lo).
Axes of the slice: x: 4, y: 4, z: 16 (z_hi: 4, z_lo: 4; z = z_hi * 4 + z_lo), core: 2. Of those that a mesh axis runs over, the one named last changes fastest.
Arguments:
- tokens: bfloat16 [49152, 768], P(('seq', 'head')), may hold values from -6 to 6
- norm_gain: float32 [768], replicated, may hold values from 0.5 to 1.5
- qkv_weight: bfloat16 [3, 12, 64, 768], P(None, 'head'), may hold values from -1 to 1
- out_weight: bfloat16 [768, 768], replicated, may hold values from -0.21875 to 0.21875
- dec_weight: bfloat16 [256, 3, 3, 768], P('head'), may hold values from -0.078125 to 0.078125
- offsets: int32 [3, 12], replicated, may hold values from 0 to 127, as said below
Outputs:
- layer: bfloat16 [49152, 768], P(('seq', 'head'))
- decoded: bfloat16 [256, 128, 384], P('head', 'seq')
Inputs may be any that keep to these rules, and one draw needn't show every extreme that they name: offsets[0, h], offsets[1, h] and offsets[2, h] lie below 4, 8 and 128 respectively; in each of the three rows some head takes that row's largest offset and some other head takes 0.
All inputs are finite; a program needn't handle non-finite values.
Results may differ from a plain program's by a relative error of at most 0.012.
Values may be sent and summed in bfloat16 or wider, within the bound.
A program may use at most 64 MiB of HBM per device.

v0:
```python
import jax
import jax.numpy as jnp
from jax import lax
from jax.sharding import PartitionSpec as P

HEAD_DIM = 64
GRID_W = 384
GROUP2 = 4
GROUP3 = 8


def partner_2(array, axis, apart):
    return lax.ppermute(array, axis, [(i, i ^ 1 << apart) for i in range(lax.axis_size(axis))])


def extended_2(block, sides, width):
    for axis, dim in sides:
        count = lax.axis_size(axis)
        forward = [(i, i + 1) for i in range(count - 1)]
        backward = [(target, source) for source, target in forward]
        low = lax.ppermute(
            lax.slice_in_dim(block, block.shape[dim] - width, None, axis=dim), axis, forward
        )
        high = lax.ppermute(lax.slice_in_dim(block, 0, width, axis=dim), axis, backward)
        block = jnp.concatenate([low, block, high], axis=dim)
    return block


def layer_norm(token_rows, norm_scale):
    values = token_rows.astype(jnp.float32)
    centred = values - jnp.mean(values, -1, keepdims=True)
    spread = jnp.mean(centred * centred, -1, keepdims=True)
    return (centred * lax.rsqrt(spread + 1e-06) * norm_scale).astype(jnp.bfloat16)


def attend(queries, key_rows, value_rows):
    scores = jnp.einsum(
        "hqd,hkd->hqk", queries, key_rows, preferred_element_type=jnp.float32
    ) * queries.shape[-1] ** (-0.5)
    row_peak = jnp.max(scores, -1, keepdims=True)
    exp_terms = jnp.exp(scores - row_peak)
    totals = jnp.sum(exp_terms, -1)
    prob_weights = exp_terms.astype(jnp.bfloat16)
    summed = jnp.einsum(
        "hqk,hkd->hqd", prob_weights, value_rows, preferred_element_type=jnp.float32
    )
    return (summed / totals[..., None], row_peak[..., 0] + jnp.log(totals))


def take_heads(projected, group, head_offsets):
    heads_here = projected.shape[2]
    shaped = projected.reshape(
        projected.shape[0] // group, group, 3, heads_here, projected.shape[3]
    )
    picked = [
        lax.dynamic_index_in_dim(
            shaped[:, :, :, index_head, :], head_offsets[index_head], 1, keepdims=False
        )
        for index_head in range(heads_here)
    ]
    return jnp.stack(picked, 0)


def split_set(chosen):
    queries = chosen[:, :, 0, :]
    key_value = chosen[:, :, 1:, :].reshape(chosen.shape[0], chosen.shape[1], 2 * chosen.shape[3])
    return (queries, key_value)


def spread_back(result, lse_rows, group, head_offsets):
    heads_here, set_rows, head_width = result.shape
    hit_marks = jnp.arange(group, dtype=jnp.int32)[None, :] == head_offsets[:, None]
    full_out = (result[:, :, None, :] * hit_marks.astype(jnp.float32)[:, None, :, None]).reshape(
        heads_here, set_rows * group, head_width
    )
    cover = jnp.broadcast_to(hit_marks[:, None, :], (heads_here, set_rows, group)).reshape(
        heads_here, set_rows * group
    )
    lse_full = jnp.broadcast_to(lse_rows[:, :, None], (heads_here, set_rows, group)).reshape(
        heads_here, set_rows * group
    )
    return (full_out, lse_full, cover)


def pair_rows(buffer_rows, pair_bits):
    for bit_level in range(pair_bits):
        partner = partner_2(buffer_rows, "seq", bit_level)
        buffer_rows = jnp.concatenate((buffer_rows, partner), 1)
    return buffer_rows


def tap_rows(block_rows, row_tap, dec_weight, model_width):
    summed = None
    for col_tap in range(3):
        window = block_rows[:, col_tap : col_tap + GRID_W, :].reshape(-1, model_width)
        term_cols = jnp.einsum(
            "cd,nd->cn",
            dec_weight[:, row_tap, col_tap, :],
            window,
            preferred_element_type=jnp.float32,
        )
        summed = term_cols if summed is None else summed + term_cols
    return summed


def project_rows(token_rows, attn_rows, out_weight):
    return (
        token_rows.astype(jnp.float32)
        + jnp.dot(attn_rows, out_weight, preferred_element_type=jnp.float32)
    ).astype(jnp.bfloat16)


def shards(tokens, norm_gain, qkv_weight, out_weight, dec_weight, offsets):
    full_rows = lax.all_gather(tokens, "head", axis=0, tiled=True)
    tok_dev = full_rows.shape[0]
    normed = layer_norm(full_rows, norm_gain)
    model_width = full_rows.shape[1]
    heads_here = qkv_weight.shape[1]
    projected = jnp.einsum(
        "td,kd->tk",
        normed,
        qkv_weight.reshape(3 * heads_here * HEAD_DIM, model_width),
        preferred_element_type=jnp.float32,
    )
    projected = projected.astype(jnp.bfloat16).reshape(tok_dev, 3, heads_here, HEAD_DIM)
    head_start = lax.axis_index("head") * heads_here
    head_offsets = lax.dynamic_slice_in_dim(offsets, head_start, heads_here, 1)
    local_q, local_kv = split_set(jnp.transpose(projected, (2, 0, 1, 3)))
    out_one, lse_one = attend(local_q, local_kv[..., :HEAD_DIM], local_kv[..., HEAD_DIM:])
    group_list = (GROUP2, GROUP3, lax.axis_size("seq"))
    query_list = []
    sent_list = []
    for branch_idx in range(3):
        branch_q, branch_kv = split_set(
            take_heads(projected, group_list[branch_idx], head_offsets[branch_idx])
        )
        query_list.append(branch_q)
        sent_list.append(branch_kv)
    bits_two = GROUP2.bit_length() - 1
    bits_three = GROUP3.bit_length() - 1
    gathered = [pair_rows(sent_list[0], bits_two), pair_rows(sent_list[1], bits_three)]
    gathered.append(lax.all_gather(sent_list[2], "seq", axis=1, tiled=True))
    spread_list = []
    for branch_idx in range(3):
        key_value = gathered[branch_idx]
        branch_out, branch_lse = attend(
            query_list[branch_idx], key_value[..., :HEAD_DIM], key_value[..., HEAD_DIM:]
        )
        spread_list.append(
            spread_back(branch_out, branch_lse, group_list[branch_idx], head_offsets[branch_idx])
        )
    peak_lse = lse_one
    for full_out, lse_full, cover in spread_list:
        peak_lse = jnp.where(cover, jnp.maximum(peak_lse, lse_full), peak_lse)
    weight_one = jnp.exp(lse_one - peak_lse)
    numerator = weight_one[..., None] * out_one
    denominator = weight_one
    for full_out, lse_full, cover in spread_list:
        weight_branch = jnp.where(
            cover, jnp.exp(jnp.where(cover, lse_full, peak_lse) - peak_lse), 0.0
        )
        numerator = numerator + weight_branch[..., None] * full_out
        denominator = denominator + weight_branch
    merged = (numerator / denominator[..., None]).astype(jnp.bfloat16)
    merged_rows = jnp.transpose(merged, (1, 0, 2)).reshape(tok_dev, heads_here * HEAD_DIM)
    attn_own = lax.all_to_all(merged_rows, "head", split_axis=0, concat_axis=1, tiled=True)
    layer_own = project_rows(tokens, attn_own, out_weight)
    layer_full = lax.all_gather(layer_own, "head", axis=0, tiled=True)
    grid_rows = tok_dev // GRID_W
    grid = layer_full.reshape(grid_rows, GRID_W, model_width)
    extended = extended_2(grid, (("seq", 0),), 1)
    padded = jnp.pad(extended, ((0, 0), (1, 1), (0, 0)))
    conv = None
    for row_tap in range(3):
        term_rows = tap_rows(
            padded[row_tap : row_tap + grid_rows], row_tap, dec_weight, model_width
        )
        conv = term_rows if conv is None else conv + term_rows
    decoded = (
        jax.nn.gelu(conv, approximate=False).astype(jnp.bfloat16).reshape(-1, grid_rows, GRID_W)
    )
    return (layer_own, decoded)


def solution(mesh):
    placed = (
        P(("seq", "head"), None),
        P(),
        P(None, "head", None, None),
        P(),
        P("head", None, None, None),
        P(),
    )
    return jax.shard_map(
        shards,
        mesh=mesh,
        in_specs=placed,
        out_specs=(P(("seq", "head"), None), P("head", "seq", None)),
        check_vma=False,
    )
```

profile of v0, /device:TPU:31, one launch (start us, length us, event | category | flops | bytes accessed | tf_op | source)
XLA Modules:
  0.0 394.9 jit_solution(5016842777074815680)
XLA Ops:
  6.3 16.1 %all_gather.9 = bf16[384,768]{1,0:T(8,128)(2,1)S(1)} all-gather(bf16[96,768]{1,0:T(8,128)(2,1)} %param.6), channel_id=1, replica_groups=mesh['seq'=128,'head'=4] {'head'}, dimensions={0}, use_global_device_ids=true | all-gather | bytes 737280 | tf_op jit(solution)/shard_map/all_gather | solution.py:114
  24.7 2.5 fusion.136
  31.5 4.6 %collective-permute-start.2 = (bf16[3,48,128]{1,2,0:T(8,128)(2,1)S(1)}, bf16[3,48,128]{1,2,0:T(8,128)(2,1)}, u32[]{:S(2)}, u32[]{:S(2)}) collective-permute-start(bf16[3,48,128]{1,2,0:T(8,128)(2,1)S(1)} %bitcast.245), channel_id=1, source_target_pairs={{0,4},{4,0},{8,12},{12,8},{16,20},{20,16},{24,28},{28,24},{32,36},... | collective-permute-start | bytes 110600 | tf_op jit(solution)/shard_map/ppermute | solution.py:13
  40.7 2.3 fusion.135
  44.2 1.3 constant_dynamic-slice_fusion.6
  47.4 1.9 collective-permute-start
  57.2 213.9 %all_gather.10 = bf16[3,384,128]{2,0,1:T(4,128)(2,1)S(1)} all-gather(bf16[3,3,128]{2,0,1:T(4,128)(2,1)S(1)} %reshape.510), channel_id=1, replica_groups=mesh['seq'=128,'head'=4] {'seq'}, dimensions={1}, use_global_device_ids=true | all-gather | bytes 297216 | tf_op jit(solution)/shard_map/all_gather | solution.py:142
  274.2 1.6 pad_maximum_fusion.6
  275.8 1.9 collective-permute-start.3
  277.8 1.7 pad_maximum_fusion.2
  279.5 3.4 collective-permute-start.1
  285.3 1.2 mul.186
  289.4 1.8 pad_maximum_fusion.3
  291.2 2.1 collective-permute-start.4
  293.3 1.2 pad_maximum_fusion
  298.3 1.2 convolution_divide_fusion.1
  302.3 1.3 pad_maximum_fusion.1
  309.1 1.7 fusion.20
  311.2 10.1 %all_to_all.19 = bf16[4,96,192]{2,1,0:T(8,128)(2,1)S(1)} all-to-all(bf16[4,96,192]{2,1,0:T(8,128)(2,1)S(1)} %copy.97), channel_id=1, replica_groups=mesh['seq'=128,'head'=4] {'head'}, dimensions={0} | all-to-all | bytes 294912 | tf_op jit(solution)/shard_map/all_to_all | solution.py:166
  322.0 14.0 %all_gather.11 = bf16[384,768]{1,0:T(8,128)(2,1)S(1)} all-gather(bf16[96,768]{1,0:T(8,128)(2,1)S(1)} %fusion.19), channel_id=1, replica_groups=mesh['seq'=128,'head'=4] {'head'}, dimensions={0}, use_global_device_ids=true | all-gather | bytes 737280 | tf_op jit(solution)/shard_map/all_gather | solution.py:168
  336.0 17.0 %collective-permute-start.5 = (bf16[1,384,768]{2,1,0:T(8,128)(2,1)S(1)}, bf16[1,384,768]{2,1,0:T(8,128)(2,1)S(1)}, u32[]{:S(2)}, u32[]{:S(2)}) collective-permute-start(bf16[1,384,768]{2,1,0:T(8,128)(2,1)S(1)} %bitcast.239), channel_id=1, source_target_pairs={{0,4},{4,8},{8,12},{12,16},{16,20},{20,24},{24,28},{28,32},{32,36}... | collective-permute-start | bytes 1769480 | tf_op jit(solution)/shard_map/ppermute | solution.py:21
  353.0 1.9 collective-permute-start.6
  355.2 4.6 %collective-permute-done.5 = bf16[1,384,768]{2,1,0:T(8,128)(2,1)S(1)} collective-permute-done((bf16[1,384,768]{2,1,0:T(8,128)(2,1)S(1)}, bf16[1,384,768]{2,1,0:T(8,128)(2,1)S(1)}, u32[]{:S(2)}, u32[]{:S(2)}) %collective-permute-start.5) | collective-permute-done | bytes 589856 | tf_op jit(solution)/shard_map/ppermute | solution.py:21
  359.9 31.2 %collective-permute-done.6 = bf16[1,384,768]{2,1,0:T(8,128)(2,1)S(1)} collective-permute-done((bf16[1,384,768]{2,1,0:T(8,128)(2,1)S(1)}, bf16[1,384,768]{2,1,0:T(8,128)(2,1)S(1)}, u32[]{:S(2)}, u32[]{:S(2)}) %collective-permute-start.6) | collective-permute-done | bytes 589856 | tf_op jit(solution)/shard_map/ppermute | solution.py:24
  (131 shorter events, 35.5 us)
Async XLA Ops:
  0.6 321.0 %copy-start = (bf16[768,768]{1,0:T(8,128)(2,1)S(1)}, bf16[768,768]{1,0:T(8,128)(2,1)}, u32[]{:S(2)}) copy-start(bf16[768,768]{1,0:T(8,128)(2,1)} %param.9) | copy-start | bytes 3538948
  0.6 22.3 %copy-start.15 = (bf16[3,3,64,768]{3,2,1,0:T(8,128)(2,1)S(1)}, bf16[3,3,64,768]{3,2,1,0:T(8,128)(2,1)}, u32[]{:S(2)}) copy-start(bf16[3,3,64,768]{3,2,1,0:T(8,128)(2,1)} %param.8) | copy-start | bytes 2654212
  0.7 22.3 %copy-start.16 = (f32[768]{0:T(1024)S(1)}, f32[768]{0:T(1024)}, u32[]{:S(2)}) copy-start(f32[768]{0:T(1024)} %param.7) | copy-start | bytes 9220
  29.6 10.4 %copy-start.8 = (bf16[48,1,3,1,64]{4,0,2,3,1:T(8,128)(2,1)}, bf16[48,1,3,1,64]{4,0,2,3,1:T(8,128)(2,1)S(1)}, u32[]{:S(2)}) copy-start(bf16[48,1,3,1,64]{4,0,2,3,1:T(8,128)(2,1)S(1)} %copy.123) | copy-start | bytes 55300
  29.6 10.4 %copy-start.9 = (bf16[48,1,3,1,64]{4,0,2,3,1:T(8,128)(2,1)}, bf16[48,1,3,1,64]{4,0,2,3,1:T(8,128)(2,1)S(1)}, u32[]{:S(2)}) copy-start(bf16[48,1,3,1,64]{4,0,2,3,1:T(8,128)(2,1)S(1)} %copy.124) | copy-start | bytes 55300
  31.3 6.6 %copy-start.10 = (bf16[48,1,3,1,64]{4,0,2,3,1:T(8,128)(2,1)}, bf16[48,1,3,1,64]{4,0,2,3,1:T(8,128)(2,1)S(1)}, u32[]{:S(2)}) copy-start(bf16[48,1,3,1,64]{4,0,2,3,1:T(8,128)(2,1)S(1)} %copy.125) | copy-start | bytes 55300
  31.5 257.9 %copy-start.1 = (bf16[3,48,2,64]{1,3,2,0:T(8,128)(2,1)}, bf16[3,48,2,64]{1,3,2,0:T(8,128)(2,1)S(1)}, u32[]{:S(2)}) copy-start(bf16[3,48,2,64]{1,3,2,0:T(8,128)(2,1)S(1)} %copy.84) | copy-start | bytes 110596
  31.5 242.7 %collective-permute-start.2 = (bf16[3,48,128]{1,2,0:T(8,128)(2,1)S(1)}, bf16[3,48,128]{1,2,0:T(8,128)(2,1)}, u32[]{:S(2)}, u32[]{:S(2)}) collective-permute-start(bf16[3,48,128]{1,2,0:T(8,128)(2,1)S(1)} %bitcast.245), channel_id=1, source_target_pairs={{0,4},{4,0},{8,12},{12,8},{16,20},{20,16},{24,28},{28,24},{32,36},... | collective-permute-start | bytes 110600 | tf_op jit(solution)/shard_map/ppermute | solution.py:13
  45.7 5.5 %copy-start.6 = (bf16[96,1,3,1,64]{0,4,3,2,1:T(8,128)(2,1)}, bf16[96,1,3,1,64]{0,4,3,2,1:T(8,128)(2,1)S(1)}, u32[]{:S(2)}) copy-start(bf16[96,1,3,1,64]{0,4,3,2,1:T(8,128)(2,1)S(1)} %copy.75) | copy-start | bytes 110596
  46.7 4.6 %copy-start.7 = (bf16[96,1,3,1,64]{0,4,3,2,1:T(8,128)(2,1)}, bf16[96,1,3,1,64]{0,4,3,2,1:T(8,128)(2,1)S(1)}, u32[]{:S(2)}) copy-start(bf16[96,1,3,1,64]{0,4,3,2,1:T(8,128)(2,1)S(1)} %copy.73) | copy-start | bytes 110596
  47.4 230.4 %collective-permute-start = (bf16[3,96,128]{1,2,0:T(8,128)(2,1)}, bf16[3,96,128]{1,2,0:T(8,128)(2,1)}, u32[]{:S(2)}, u32[]{:S(2)}) collective-permute-start(bf16[3,96,128]{1,2,0:T(8,128)(2,1)} %bitcast.19), channel_id=1, source_target_pairs={{0,4},{4,0},{8,12},{12,8},{16,20},{20,16},{24,28},{28,24},{32,36},... | collective-permute-start | bytes 221192 | tf_op jit(solution)/shard_map/ppermute | solution.py:13
  271.4 1.7 copy-start.14
  272.7 1.5 copy-start.2
  275.8 13.5 %collective-permute-start.3 = (bf16[3,96,128]{1,2,0:T(8,128)(2,1)}, bf16[3,96,128]{1,2,0:T(8,128)(2,1)}, u32[]{:S(2)}, u32[]{:S(2)}) collective-permute-start(bf16[3,96,128]{1,2,0:T(8,128)(2,1)} %pad_maximum_fusion.6), channel_id=1, source_target_pairs={{0,8},{4,12},{8,0},{12,4},{16,24},{20,28},{24,16},{28,20},{32,40},... | collective-permute-start | bytes 221192 | tf_op jit(solution)/shard_map/ppermute | solution.py:13
  279.5 13.8 %collective-permute-start.1 = (bf16[3,192,128]{1,2,0:T(8,128)(2,1)}, bf16[3,192,128]{1,2,0:T(8,128)(2,1)}, u32[]{:S(2)}, u32[]{:S(2)}) collective-permute-start(bf16[3,192,128]{1,2,0:T(8,128)(2,1)} %pad_maximum_fusion.2), channel_id=1, source_target_pairs={{0,8},{4,12},{8,0},{12,4},{16,24},{20,28},{24,16},{28,20},{32,40},... | collective-permute-start | bytes 442376 | tf_op jit(solution)/shard_map/ppermute | solution.py:13
  291.2 11.1 %collective-permute-start.4 = (bf16[3,192,128]{1,2,0:T(8,128)(2,1)}, bf16[3,192,128]{1,2,0:T(8,128)(2,1)}, u32[]{:S(2)}, u32[]{:S(2)}) collective-permute-start(bf16[3,192,128]{1,2,0:T(8,128)(2,1)} %pad_maximum_fusion.3), channel_id=1, source_target_pairs={{0,16},{4,20},{8,24},{12,28},{16,0},{20,4},{24,8},{28,12},{32,48},... | collective-permute-start | bytes 442376 | tf_op jit(solution)/shard_map/ppermute | solution.py:13
  294.5 0.7 copy-start.3
  296.3 0.6 copy-start.12
  296.9 0.6 copy-start.13
  310.8 10.8 %copy-start.4 = (bf16[96,768]{1,0:T(8,128)(2,1)S(1)}, bf16[96,768]{1,0:T(8,128)(2,1)}, u32[]{:S(2)}) copy-start(bf16[96,768]{1,0:T(8,128)(2,1)} %param.6) | copy-start | bytes 442372
  311.2 43.8 %copy-start.11 = (bf16[64,3,3,768]{3,0,2,1:T(8,128)(2,1)S(1)}, bf16[64,3,3,768]{3,0,2,1:T(8,128)(2,1)}, u32[]{:S(2)}) copy-start(bf16[64,3,3,768]{3,0,2,1:T(8,128)(2,1)} %param.10) | copy-start | bytes 2654212
  322.0 69.5 %copy-start.5 = (bf16[96,768]{1,0:T(8,128)(2,1)}, bf16[96,768]{1,0:T(8,128)(2,1)S(1)}, u32[]{:S(2)}) copy-start(bf16[96,768]{1,0:T(8,128)(2,1)S(1)} %fusion.19) | copy-start | bytes 442372
  336.0 23.9 %collective-permute-start.5 = (bf16[1,384,768]{2,1,0:T(8,128)(2,1)S(1)}, bf16[1,384,768]{2,1,0:T(8,128)(2,1)S(1)}, u32[]{:S(2)}, u32[]{:S(2)}) collective-permute-start(bf16[1,384,768]{2,1,0:T(8,128)(2,1)S(1)} %bitcast.239), channel_id=1, source_target_pairs={{0,4},{4,8},{8,12},{12,16},{16,20},{20,24},{24,28},{28,32},{32,36}... | collective-permute-start | bytes 1769480 | tf_op jit(solution)/shard_map/ppermute | solution.py:21
  353.0 38.1 %collective-permute-start.6 = (bf16[1,384,768]{2,1,0:T(8,128)(2,1)S(1)}, bf16[1,384,768]{2,1,0:T(8,128)(2,1)S(1)}, u32[]{:S(2)}, u32[]{:S(2)}) collective-permute-start(bf16[1,384,768]{2,1,0:T(8,128)(2,1)S(1)} %bitcast.240), channel_id=1, source_target_pairs={{4,0},{8,4},{12,8},{16,12},{20,16},{24,20},{28,24},{32,28},{36,32}... | collective-permute-start | bytes 1769480 | tf_op jit(solution)/shard_map/ppermute | solution.py:24
where the time goes:
time: 396 us; the launch traced here: 395 us
  blocking collectives  254 us (64%)
  waiting for transfers between devices  35.8 us (9%)
  starting transfers between devices  32.7 us (8%)
  local copies, waits for them, and re-layouts  31 us (8%)
  between operations  18.9 us (5%)
  matrix products  11.6 us (3%)
  other arithmetic  10.6 us (3%)
    all_gather x1, blocking collectives, shards(): gathered.append(lax.all_gather(sent_list[2], 'seq', axis=1, tiled=True))  214 us
    ppermute x1, waiting for transfers between devices, extended_2(): lax.ppermute(lax.slice_in_dim(block, 0, width, axis=dim), axis, backward)  31.2 us
    ppermute x1, starting transfers between devices, extended_2(): lax.ppermute(lax.slice_in_dim(block, block.shape[dim] - width, None, axis...  17 us
    all_gather x1, blocking collectives, shards(): full_rows = lax.all_gather(tokens, 'head', axis=0, tiled=True)  16.1 us
    all_gather x1, blocking collectives, shards(): layer_full = lax.all_gather(layer_own, 'head', axis=0, tiled=True)  14 us
    ppermute x5, starting transfers between devices, partner_2(): lax.ppermute(array, axis, [(i, i ^ 1 << apart) for i in range(lax.axis_si...  13.8 us
    all_to_all x1, blocking collectives, shards(): lax.all_to_all(merged_rows, 'head', split_axis=0, concat_axis=1, tiled=True)  10.1 us
  transfers between devices with their start and end apart: 7, of which 2 were waited for; matrix products, arithmetic and copies ran while one was open for 8% of the time, Pallas kernels for 0%

commit v1 on v0

v1 whole, which is shorter than its diff:
```python
import functools

import jax
import jax.numpy as jnp
from jax import lax
from jax.experimental import pallas as pl
from jax.experimental.pallas import tpu as pltpu
from jax.sharding import PartitionSpec as P

MESH = pl.DeviceIdType.MESH
LOG2E = 1.4426950408889634
SCALE = 0.125 * LOG2E
F32 = jnp.float32
BF16 = jnp.bfloat16


def nt_dot(a, b):
    return lax.dot_general(a, b, (((1,), (1,)), ((), ())), preferred_element_type=F32)


def seq_of(zh, x, y, c):
    return ((zh * 4 + x) * 4 + y) * 2 + c


def layer_norm(rows, gain):
    values = rows.astype(F32)
    centred = values - jnp.mean(values, -1, keepdims=True)
    spread = jnp.mean(centred * centred, -1, keepdims=True)
    return (centred * lax.rsqrt(spread + 1e-06) * gain).astype(BF16)


def attend(q, kv, out_lanes, keep=None):
    scores = nt_dot(q, kv) * SCALE
    if keep is not None:
        scores = jnp.where(keep, scores, -1e30)
    top = jnp.max(scores, -1, keepdims=True)
    terms = jnp.exp2(scores - top)
    total = jnp.sum(terms, -1, keepdims=True)
    out = jnp.dot(terms.astype(BF16), kv, preferred_element_type=F32)
    lse = top + jnp.log(total) * LOG2E
    return jnp.where(out_lanes, out / total, lse)


def body(
    tok, gain, wqkv, wout, wdec, off,
    layer_out, dec_out,
    X, gain_v, WQ, W01, W2, WD, QB, QF,
    S2, B2, S3, B3, S4F, Q4F, G1, G2,
    T1, E2, E3, MR, A01, A2, PF, PT, L, HS, HR, DO,
    in_sem, tok_s, tok_r, b2_s, b2_r, b3_s, b3_r, g1_s, g1_r, g2_s, g2_r,
    a01_s, a01_r, a2_s, a2_r, pt_s, pt_r, h_s, h_r, out_sem,
):
    s = lax.axis_index("seq")
    z = lax.axis_index("head")
    core = lax.rem(s, 2)
    y = lax.rem(lax.div(s, 2), 4)
    x = lax.rem(lax.div(s, 8), 4)
    zh = lax.div(s, 32)
    yc = lax.rem(s, 8)
    zx = lax.div(s, 8)
    quad = lax.rem(s, 4)

    def head_peer(d):
        return (s, lax.rem(z + d, 4))

    def quad_peer(d):
        return (s - quad + lax.rem(quad + d, 4), z)

    def yc_peer(d):
        return (s - yc + lax.rem(yc + d, 8), z)

    def zx_peer(d):
        return (lax.rem(zx + d, 16) * 8 + yc, z)

    up = (lax.rem(s + 1, 128), z)
    down = (lax.rem(s + 127, 128), z)

    barrier = pltpu.get_barrier_semaphore()
    peers = [head_peer(d) for d in range(1, 4)]
    peers += [yc_peer(d) for d in range(1, 8)]
    peers += [zx_peer(d) for d in range(1, 16)]
    peers += [up, down]
    for peer in peers:
        pl.semaphore_signal(barrier, inc=1, device_id=peer, device_id_type=MESH)

    loads = []

    def load(src, dst):
        copy = pltpu.make_async_copy(src, dst, in_sem.at[len(loads)])
        copy.start()
        loads.append(copy)
        return copy

    c_tok = load(tok, X.at[z])
    c_gain = load(gain, gain_v)
    c_qkv = []
    for h in range(3):
        q_at, k_at, v_at = (64, 64, 0) if h == 0 else (0, 0, 64)
        c_qkv.append(load(wqkv.at[pl.ds(64 * h, 64)], WQ.at[pl.ds(128 * h + q_at, 64)]))
        c_qkv.append(load(wqkv.at[pl.ds(192 + 64 * h, 64)], WQ.at[pl.ds(384 + 128 * h + k_at, 64)]))
        c_qkv.append(load(wqkv.at[pl.ds(384 + 64 * h, 64)], WQ.at[pl.ds(384 + 128 * h + v_at, 64)]))
    c_late = [load(wdec, WD)]
    for g in range(4):
        c_late.append(load(wout.at[pl.ds(192 * g, 128)], W01.at[pl.ds(128 * g, 128)]))
        c_late.append(load(wout.at[pl.ds(192 * g + 128, 64)], W2.at[0, pl.ds(128 * g, 64)]))
        c_late.append(load(wout.at[pl.ds(192 * g + 128, 64)], W2.at[1, pl.ds(128 * g + 64, 64)]))
    zero64 = jnp.zeros((64, 768), BF16)
    for h in range(3):
        WQ[pl.ds(128 * h + (0 if h == 0 else 64), 64), :] = zero64
    for g in range(4):
        W2[0, pl.ds(128 * g + 64, 64), :] = zero64
        W2[1, pl.ds(128 * g, 64), :] = zero64
    S4F[...] = jnp.zeros_like(S4F)
    Q4F[...] = jnp.zeros_like(Q4F)

    c_tok.wait()
    pl.semaphore_wait(barrier, len(peers))

    def remote(src, dst, ssem, rsem, peer):
        return pltpu.make_async_remote_copy(
            src_ref=src, dst_ref=dst, send_sem=ssem, recv_sem=rsem,
            device_id=peer, device_id_type=MESH,
        )

    sent = []

    tok_copies = [
        remote(X.at[z], X.at[z], tok_s.at[d], tok_r.at[d], head_peer(d)) for d in range(1, 4)
    ]
    for copy in tok_copies:
        copy.start()
    sent += tok_copies

    c_gain.wait()
    for copy in c_qkv:
        copy.wait()
    gain_row = gain_v[...]

    for d in range(4):
        src = lax.rem(z - d + 4, 4)
        if d:
            remote(X.at[src], X.at[src], tok_s.at[d], tok_r.at[d], head_peer(d)).wait_recv()
        normed = layer_norm(X[src], gain_row)
        rows = pl.ds(pl.multiple_of(src * 96, 96), 96)
        for t in range(6):
            part = nt_dot(normed, WQ[pl.ds(128 * t, 128), :]).astype(BF16)
            QB[t, rows, :] = part
            QF[t, rows, :] = part.astype(F32)

    lane = lax.broadcasted_iota(jnp.int32, (1, 128), 1)
    left = lane < 64
    right = lane >= 64
    out_lanes = (left, right, right)
    o2 = [off[0, 3 * z + h] for h in range(3)]
    o3 = [off[1, 3 * z + h] for h in range(3)]
    o4 = [off[2, 3 * z + h] for h in range(3)]

    for h in range(3):
        for j in range(3):
            S4F[3 * h + j : 3 * h + j + 1, :] = QF[3 + h, pl.ds(o4[h] + 128 * j, 1), :]
            Q4F[3 * h + j : 3 * h + j + 1, :] = QF[h, pl.ds(o4[h] + 128 * j, 1), :]
    G1[zx] = S4F[...].astype(BF16)
    g1_copies = [
        remote(G1.at[zx], G1.at[zx], g1_s.at[d], g1_r.at[d], zx_peer(d)) for d in range(1, 16)
    ]
    for copy in g1_copies:
        copy.start()
    for h in range(3):
        B2[quad, h] = QF[3 + h, pl.ds(o2[h], 96, stride=4), :].astype(BF16)
        B3[yc, h] = QF[3 + h, pl.ds(o3[h], 48, stride=8), :].astype(BF16)
    b2_copies = [
        remote(B2.at[quad], B2.at[quad], b2_s.at[d], b2_r.at[d], quad_peer(d)) for d in range(1, 4)
    ]
    b3_copies = [
        remote(B3.at[yc], B3.at[yc], b3_s.at[d], b3_r.at[d], yc_peer(d)) for d in range(1, 8)
    ]
    for copy in b2_copies + b3_copies:
        copy.start()
    sent += g1_copies + b2_copies + b3_copies

    def branch_one(h):
        kv = QB[3 + h]
        for i in range(3):
            rows = pl.ds(128 * i, 128)
            T1[h, rows, :] = attend(QB[h, rows, :], kv, out_lanes[h])

    branch_one(0)
    branch_one(1)

    for d in range(1, 16):
        src = lax.rem(zx - d + 16, 16)
        remote(G1.at[src], G1.at[src], g1_s.at[d], g1_r.at[d], zx_peer(d)).wait_recv()
    G2[yc] = G1[...]
    g2_copies = [
        remote(G2.at[yc], G2.at[yc], g2_s.at[d], g2_r.at[d], yc_peer(d)) for d in range(1, 8)
    ]
    for copy in g2_copies:
        copy.start()
    sent += g2_copies

    branch_one(2)

    for d in range(1, 4):
        src = lax.rem(quad - d + 4, 4)
        remote(B2.at[src], B2.at[src], b2_s.at[d], b2_r.at[d], quad_peer(d)).wait_recv()

    for h in range(3):
        kv = jnp.concatenate([B2[m, h] for m in range(4)], axis=0)
        q = QF[h, pl.ds(o2[h], 96, stride=4), :].astype(BF16)
        tile = attend(q, kv, out_lanes[h])
        for p in range(4):
            E2[h, pl.ds(p, 96, stride=4), :] = tile

    for d in range(1, 8):
        src = lax.rem(yc - d + 8, 8)
        remote(B3.at[src], B3.at[src], b3_s.at[d], b3_r.at[d], yc_peer(d)).wait_recv()

    def branch_three(h):
        kv = jnp.concatenate([B3[m, h] for m in range(8)], axis=0)
        q = QF[h, pl.ds(o3[h], 48, stride=8), :].astype(BF16)
        tile = attend(q, kv, out_lanes[h])
        for p in range(8):
            E3[h, pl.ds(p, 48, stride=8), :] = tile

    token = lax.broadcasted_iota(jnp.int32, (384, 128), 0)

    def merge(h):
        t1, t2, t3 = T1[h], E2[h], E3[h]
        l1, l2, l3 = (pltpu.roll(t, 64, 1) for t in (t1, t2, t3))
        c2 = (token & 3) == o2[h]
        c3 = (token & 7) == o3[h]
        peak = jnp.where(c2, jnp.maximum(l1, l2), l1)
        peak = jnp.where(c3, jnp.maximum(peak, l3), peak)
        w1 = jnp.exp2(l1 - peak)
        w2 = jnp.where(c2, jnp.exp2(l2 - peak), 0.0)
        w3 = jnp.where(c3, jnp.exp2(l3 - peak), 0.0)
        den = w1 + w2 + w3
        out = (w1 * t1 + w2 * t2 + w3 * t3) / den
        lse = peak + jnp.log(den) * LOG2E
        MR[h] = jnp.where(out_lanes[h], out, pltpu.roll(lse, 64, 1))
        return out

    branch_three(0)
    branch_three(1)
    A01[z] = jnp.where(left, merge(0), merge(1)).astype(BF16)
    a01_copies = [
        remote(A01.at[z], A01.at[z], a01_s.at[d], a01_r.at[d], head_peer(d)) for d in range(1, 4)
    ]
    for copy in a01_copies:
        copy.start()
    branch_three(2)
    m2 = merge(2)
    A2[z] = jnp.where(left, pltpu.roll(m2[:192], 64, 1), m2[192:]).astype(BF16)
    a2_copies = [
        remote(A2.at[z], A2.at[z], a2_s.at[d], a2_r.at[d], head_peer(d)) for d in range(1, 4)
    ]
    for copy in a2_copies:
        copy.start()
    sent += a01_copies + a2_copies

    for d in range(1, 8):
        src = lax.rem(yc - d + 8, 8)
        remote(G2.at[src], G2.at[src], g2_s.at[d], g2_r.at[d], yc_peer(d)).wait_recv()
    kv4 = G2[...].reshape(2048, 128)
    key_row = lax.broadcasted_iota(jnp.int32, (16, 2048), 1) & 15
    query_row = lax.broadcasted_iota(jnp.int32, (16, 2048), 0)

    def head_row(r):
        return jnp.where(r < 3, 0, jnp.where(r < 6, 1, jnp.where(r < 9, 2, 3)))

    keep = head_row(key_row) == head_row(query_row)
    row16 = lax.broadcasted_iota(jnp.int32, (16, 128), 0)
    lane16 = lax.broadcasted_iota(jnp.int32, (16, 128), 1)
    out16 = (row16 < 3) == (lane16 < 64)
    tile4 = attend(Q4F[...].astype(BF16), kv4, out16, keep)
    for h in range(3):
        for j in range(3):
            S4F[3 * h + j : 3 * h + j + 1, :] = MR[h, pl.ds(o4[h] + 128 * j, 1), :]
    tile1 = S4F[...]
    l1 = pltpu.roll(tile1, 64, 1)
    l4 = pltpu.roll(tile4, 64, 1)
    peak = jnp.maximum(l1, l4)
    w1 = jnp.exp2(l1 - peak)
    w4 = jnp.exp2(l4 - peak)
    both = (w1 * tile1 + w4 * tile4) / (w1 + w4)
    turned = pltpu.roll(both, 64, 1)
    PF[...] = jnp.zeros_like(PF)
    PF[0:3, :] = jnp.where(left, both[0:3], both[3:6])
    PF[3:6, :] = jnp.where(left, turned[6:9], both[6:9])
    PT[z] = PF[...].astype(BF16)
    pt_copies = [
        remote(PT.at[z], PT.at[z], pt_s.at[d], pt_r.at[d], head_peer(d)) for d in range(1, 4)
    ]
    for copy in pt_copies:
        copy.start()
    sent += pt_copies

    for copy in c_late:
        copy.wait()

    for d in range(1, 4):
        src = lax.rem(z - d + 4, 4)
        remote(A01.at[src], A01.at[src], a01_s.at[d], a01_r.at[d], head_peer(d)).wait_recv()
        remote(A2.at[src], A2.at[src], a2_s.at[d], a2_r.at[d], head_peer(d)).wait_recv()
        remote(PT.at[src], PT.at[src], pt_s.at[d], pt_r.at[d], head_peer(d)).wait_recv()
    row128 = lax.broadcasted_iota(jnp.int32, (128, 128), 0)
    tok2 = lax.broadcasted_iota(jnp.int32, (192, 128), 0) + jnp.where(left, 0, 192)
    p01, p2 = [], []
    for g in range(4):
        patch = PT[g].astype(F32)
        o_lane = jnp.where(left, off[2, 3 * g], off[2, 3 * g + 1])
        hit = row128 == o_lane
        whole = A01[g].astype(F32)
        p01.append(
            jnp.concatenate(
                [
                    jnp.where(hit, patch[j : j + 1], whole[128 * j : 128 * j + 128])
                    for j in range(3)
                ],
                axis=0,
            ).astype(BF16)
        )
        packed = A2[g].astype(F32)
        for j in range(3):
            packed = jnp.where(tok2 == off[2, 3 * g + 2] + 128 * j, patch[3 + j : 4 + j], packed)
        p2.append(packed.astype(BF16))
    for half in range(2):
        first = jnp.concatenate([p[192 * half : 192 * half + 192] for p in p01], axis=1)
        second = jnp.concatenate(p2, axis=1)
        acc = jnp.dot(first, W01[...], preferred_element_type=F32)
        acc = acc + jnp.dot(second, W2[half], preferred_element_type=F32)
        own = X[2 * half : 2 * half + 2].reshape(192, 768).astype(F32)
        L[192 * half : 192 * half + 192, :] = (own + acc).astype(BF16)
    c_layer = pltpu.make_async_copy(
        L.at[pl.ds(pl.multiple_of(z * 96, 96), 96)], layer_out, out_sem.at[0]
    )
    c_layer.start()

    col = lax.broadcasted_iota(jnp.int32, (64, 384), 1)

    def part(dy):
        p = nt_dot(WD[192 * dy : 192 * dy + 192, :], L[...])
        before = jnp.where(col == 0, 0.0, pltpu.roll(p[0:64], 1, 1))
        after = jnp.where(col == 383, 0.0, pltpu.roll(p[128:192], 383, 1))
        return before + p[64:128] + after

    HS[0] = part(0).astype(BF16)
    h_up = remote(HS.at[0], HR.at[0], h_s.at[0], h_r.at[0], up)
    h_up.start()
    HS[1] = part(2).astype(BF16)
    h_down = remote(HS.at[1], HR.at[1], h_s.at[1], h_r.at[1], down)
    h_down.start()
    middle = part(1)
    h_up.wait_recv()
    h_down.wait_recv()
    conv = middle + jnp.where(s > 0, HR[0].astype(F32), 0.0)
    conv = conv + jnp.where(s < 127, HR[1].astype(F32), 0.0)
    DO[...] = (0.5 * conv * (1.0 + lax.erf(conv * 0.7071067811865476))).astype(BF16)
    c_dec = pltpu.make_async_copy(DO, dec_out, out_sem.at[1])
    c_dec.start()

    for copy in sent + [h_up, h_down]:
        copy.wait_send()
    c_layer.wait()
    c_dec.wait()


def shards(tokens, norm_gain, qkv_weight, out_weight, dec_weight, offsets):
    wqkv = qkv_weight.reshape(576, 768)
    wdec = jnp.transpose(dec_weight, (1, 2, 0, 3)).reshape(576, 768)
    gain = norm_gain.reshape(1, 768)
    vm = pltpu.VMEM
    dma = pltpu.SemaphoreType.DMA
    layer, decoded = pl.pallas_call(
        body,
        out_shape=(
            jax.ShapeDtypeStruct((96, 768), BF16),
            jax.ShapeDtypeStruct((64, 384), BF16),
        ),
        in_specs=[pl.BlockSpec(memory_space=pl.ANY)] * 5
        + [pl.BlockSpec(memory_space=pltpu.SMEM)],
        out_specs=(pl.BlockSpec(memory_space=pl.ANY),) * 2,
        scratch_shapes=[
            vm((4, 96, 768), BF16),
            vm((1, 768), F32),
            vm((768, 768), BF16),
            vm((512, 768), BF16),
            vm((2, 512, 768), BF16),
            vm((576, 768), BF16),
            vm((6, 384, 128), BF16),
            vm((6, 384, 128), F32),
            vm((16, 128), BF16),
            vm((4, 3, 96, 128), BF16),
            vm((16, 128), BF16),
            vm((8, 3, 48, 128), BF16),
            vm((16, 128), F32),
            vm((16, 128), F32),
            vm((16, 16, 128), BF16),
            vm((8, 16, 16, 128), BF16),
            vm((3, 384, 128), F32),
            vm((3, 384, 128), F32),
            vm((3, 384, 128), F32),
            vm((3, 384, 128), F32),
            vm((4, 384, 128), BF16),
            vm((4, 192, 128), BF16),
            vm((16, 128), F32),
            vm((4, 16, 128), BF16),
            vm((384, 768), BF16),
            vm((2, 64, 384), BF16),
            vm((2, 64, 384), BF16),
            vm((64, 384), BF16),
            dma((24,)),
            dma((4,)), dma((4,)),
            dma((4,)), dma((4,)),
            dma((8,)), dma((8,)),
            dma((16,)), dma((16,)),
            dma((8,)), dma((8,)),
            dma((4,)), dma((4,)),
            dma((4,)), dma((4,)),
            dma((4,)), dma((4,)),
            dma((2,)), dma((2,)),
            dma((2,)),
        ],
        compiler_params=pltpu.CompilerParams(
            collective_id=0, has_side_effects=True, vmem_limit_bytes=48 * 1024 * 1024
        ),
        cost_estimate=pl.CostEstimate(
            flops=1500000000, bytes_accessed=4000000, transcendentals=700000
        ),
        name="dilated_layer",
    )(tokens, gain, wqkv, out_weight, wdec, offsets)
    return layer, decoded.reshape(64, 1, 384)


def solution(mesh):
    placed = (
        P(("seq", "head"), None),
        P(),
        P(None, "head", None, None),
        P(),
        P("head", None, None, None),
        P(),
    )
    return jax.shard_map(
        shards,
        mesh=mesh,
        in_specs=placed,
        out_specs=(P(("seq", "head"), None), P("head", "seq", None)),
        check_vma=False,
    )
```

time: 396 us -> 73.2 us (0.18)
  the two profiles are of different devices: /device:TPU:31 before, /device:TPU:95 now
where the time goes in v1:
time: 73.2 us; the launch traced here: 72.9 us
  Pallas kernels  65.1 us (89%)
  local copies, waits for them, and re-layouts  7.17 us (10%)
    pallas_call x1, Pallas kernels, shards(): pl.pallas_call(body, out_shape=(jax.ShapeDtypeStruct((96, 768), BF16), ja...  65.1 us
    unnamed x12, local copies, waits for them, and re-layouts  6.48 us

profile of v1, /device:TPU:95, one launch (start us, length us, event | category | flops | bytes accessed | tf_op | source)
XLA Modules:
  0.0 72.9 jit_solution(9839277985657699352)
XLA Ops:
  0.6 0.7 reshape.16.gain
  1.3 0.0 copy-start
  1.3 1.3 %copy-done = bf16[768,768]{1,0:T(8,128)(2,1)S(1)} copy-done((bf16[768,768]{1,0:T(8,128)(2,1)S(1)}, bf16[768,768]{1,0:T(8,128)(2,1)}, u32[]{:S(2)}) %copy-start) | copy-done | bytes 1179672
  2.6 0.0 copy-start.1
  2.6 1.2 %copy-done.1 = bf16[3,3,64,768]{3,2,1,0:T(8,128)(2,1)S(1)} copy-done((bf16[3,3,64,768]{3,2,1,0:T(8,128)(2,1)S(1)}, bf16[3,3,64,768]{3,2,1,0:T(8,128)(2,1)}, u32[]{:S(2)}) %copy-start.1) | copy-done | bytes 884760
  3.8 0.0 copy-start.2
  3.8 1.2 %copy-done.2 = bf16[64,3,3,768]{3,0,2,1:T(8,128)(2,1)S(1)} copy-done((bf16[64,3,3,768]{3,0,2,1:T(8,128)(2,1)S(1)}, bf16[64,3,3,768]{3,0,2,1:T(8,128)(2,1)}, u32[]{:S(2)}) %copy-start.2) | copy-done | bytes 884760
  4.9 0.0 copy-start.3
  4.9 0.9 %copy-done.3 = bf16[96,768]{1,0:T(8,128)(2,1)S(1)} copy-done((bf16[96,768]{1,0:T(8,128)(2,1)S(1)}, bf16[96,768]{1,0:T(8,128)(2,1)}, u32[]{:S(2)}) %copy-start.3) | copy-done | bytes 147480
  5.8 0.0 copy-start.4
  5.8 0.7 copy-done.4
  6.5 65.1 %dilated_layer.1 = (bf16[96,768]{1,0:T(8,128)(2,1)S(1)}, bf16[64,384]{1,0:T(8,128)(2,1)S(1)}) custom-call(bf16[96,768]{1,0:T(8,128)(2,1)S(1)} %copy-done.3, f32[1,768]{1,0:T(1,128)S(1)} %reshape.16.gain, bf16[576,768]{1,0:T(8,128)(2,1)S(1)} %bitcast.6, bf16[768,768]{1,0:T(8,128)(2,1)S(1)} %copy-done, bf16[576,768]{1,0:T(8,128)(2,1)S(1)} %bitcast.7, ...), custom_call_target="tpu_custom_call" | custom-call | flops 1500000000 | bytes 4000000 | tf_op jit(solution)/shard_map/dilated_layer/pallas_call | solution.py:374
  71.6 0.7 copy.10
  72.3 0.6 copy.11
Async XLA Ops:
  1.3 1.3 %copy-start = (bf16[768,768]{1,0:T(8,128)(2,1)S(1)}, bf16[768,768]{1,0:T(8,128)(2,1)}, u32[]{:S(2)}) copy-start(bf16[768,768]{1,0:T(8,128)(2,1)} %wout.1) | copy-start | bytes 3538948
  2.6 1.2 %copy-start.1 = (bf16[3,3,64,768]{3,2,1,0:T(8,128)(2,1)S(1)}, bf16[3,3,64,768]{3,2,1,0:T(8,128)(2,1)}, u32[]{:S(2)}) copy-start(bf16[3,3,64,768]{3,2,1,0:T(8,128)(2,1)} %param.8) | copy-start | bytes 2654212
  3.8 1.2 %copy-start.2 = (bf16[64,3,3,768]{3,0,2,1:T(8,128)(2,1)S(1)}, bf16[64,3,3,768]{3,0,2,1:T(8,128)(2,1)}, u32[]{:S(2)}) copy-start(bf16[64,3,3,768]{3,0,2,1:T(8,128)(2,1)} %param.10) | copy-start | bytes 2654212
  4.9 0.9 %copy-start.3 = (bf16[96,768]{1,0:T(8,128)(2,1)S(1)}, bf16[96,768]{1,0:T(8,128)(2,1)}, u32[]{:S(2)}) copy-start(bf16[96,768]{1,0:T(8,128)(2,1)} %tok.1) | copy-start | bytes 442372
  5.8 0.7 copy-start.4

commit v2 on v1

v2 whole, which is shorter than its diff:
```python
import functools

import jax
import jax.numpy as jnp
from jax import lax
from jax.experimental import pallas as pl
from jax.experimental.pallas import tpu as pltpu
from jax.sharding import PartitionSpec as P

MESH = pl.DeviceIdType.MESH
LOG2E = 1.4426950408889634
SCALE = 0.125 * LOG2E
F32 = jnp.float32
BF16 = jnp.bfloat16


def nt_dot(a, b):
    return lax.dot_general(a, b, (((1,), (1,)), ((), ())), preferred_element_type=F32)


def seq_of(zh, x, y, c):
    return ((zh * 4 + x) * 4 + y) * 2 + c


def layer_norm(rows, gain):
    values = rows.astype(F32)
    centred = values - jnp.mean(values, -1, keepdims=True)
    spread = jnp.mean(centred * centred, -1, keepdims=True)
    return (centred * lax.rsqrt(spread + 1e-06) * gain).astype(BF16)


def attend(q, kv, out_lanes, keep=None):
    scores = nt_dot(q, kv) * SCALE
    if keep is not None:
        scores = jnp.where(keep, scores, -1e30)
    top = jnp.max(scores, -1, keepdims=True)
    terms = jnp.exp2(scores - top)
    total = jnp.sum(terms, -1, keepdims=True)
    out = jnp.dot(terms.astype(BF16), kv, preferred_element_type=F32)
    lse = top + jnp.log(total) * LOG2E
    return jnp.where(out_lanes, out / total, lse)


def body(
    tok, gain, wqkv, wout, wdec, off,
    layer_out, dec_out,
    X, gain_v, WQ, W01, W2, WD, QB, QF,
    BX, S4F, Q4F, G1, G2,
    T1, E2, E3, MR, AA, PF, PT, L, HS, HR, DO,
    in_sem, tok_s, tok_f, tok_r, bx_s, bx_r, g1_s, g1_r, g2_s, g2_r,
    aa_s, aa_f, aa_r, pt_s, pt_r, h_s, h_r, out_sem, lead_sem, go_sem,
):
    s = lax.axis_index("seq")
    z = lax.axis_index("head")
    yc = lax.rem(s, 8)
    zx = lax.div(s, 8)
    quad = lax.rem(s, 4)
    quad_base = yc - quad
    far_base = lax.rem(quad_base + 4, 8)
    s_base = s - yc
    side = lax.div(z, 2)
    u = z + side * (3 - 2 * z)
    inner = (s, z + 1 - 2 * side)
    outer = (s, z - 1 + 2 * side)
    order = [0]
    for k, near in ((1, 1 - u), (2, 2), (3, 3)):
        order.append(near + side * (3 - 2 * near))

    def head_peer(d):
        return (s, lax.rem(z + d, 4))

    def yc_peer(d):
        return (s_base + lax.rem(yc + d, 8), z)

    def zx_peer(d):
        return (lax.rem(zx + d, 16) * 8 + yc, z)

    up = (lax.rem(s + 1, 128), z)
    down = (lax.rem(s + 127, 128), z)

    x = lax.rem(zx, 4)
    barrier = pltpu.get_barrier_semaphore()

    def signal(sem, peer):
        pl.semaphore_signal(sem, inc=1, device_id=peer, device_id_type=MESH)

    def from_lead(x_at, yc_at, z_at):
        return (x_at - z_at) * (x_at - z_at) + (yc_at - z_at) * (yc_at - z_at)

    def x_peer(d):
        return ((zx - x + lax.rem(x + d, 4)) * 8 + yc, z)

    def far_lead(d):
        return (lax.rem(zx + 4 * d, 16) * 8 + yc, z)

    greeted = [(head_peer(d), from_lead(x, yc, lax.rem(z + d, 4))) for d in range(1, 4)]
    greeted += [(yc_peer(d), from_lead(x, lax.rem(yc + d, 8), z)) for d in range(1, 8)]
    greeted += [(x_peer(d), from_lead(lax.rem(x + d, 4), yc, z)) for d in range(1, 4)]
    mine = from_lead(x, yc, z)
    for peer, gap in greeted:
        @pl.when(gap != 0)
        def _():
            signal(barrier, peer)

    loads = []

    def load(src, dst):
        copy = pltpu.make_async_copy(src, dst, in_sem.at[len(loads)])
        copy.start()
        loads.append(copy)
        return copy

    c_tok = [load(tok.at[pl.ds(48 * i, 48)], X.at[z, i]) for i in range(2)]
    c_gain = load(gain, gain_v)
    c_qkv = []
    for h in range(3):
        q_at, k_at, v_at = (64, 64, 0) if h == 0 else (0, 0, 64)
        c_qkv.append(load(wqkv.at[pl.ds(64 * h, 64)], WQ.at[pl.ds(128 * h + q_at, 64)]))
        c_qkv.append(load(wqkv.at[pl.ds(192 + 64 * h, 64)], WQ.at[pl.ds(384 + 128 * h + k_at, 64)]))
        c_qkv.append(load(wqkv.at[pl.ds(384 + 64 * h, 64)], WQ.at[pl.ds(384 + 128 * h + v_at, 64)]))
    c_late = [load(wdec, WD)]
    for g in range(4):
        c_late.append(load(wout.at[pl.ds(192 * g, 128)], W01.at[pl.ds(128 * g, 128)]))
        c_late.append(load(wout.at[pl.ds(192 * g + 128, 64)], W2.at[0, pl.ds(128 * g, 64)]))
        c_late.append(load(wout.at[pl.ds(192 * g + 128, 64)], W2.at[1, pl.ds(128 * g + 64, 64)]))
    zero64 = jnp.zeros((64, 768), BF16)
    for h in range(3):
        WQ[pl.ds(128 * h + (0 if h == 0 else 64), 64), :] = zero64
    for g in range(4):
        W2[0, pl.ds(128 * g + 64, 64), :] = zero64
        W2[1, pl.ds(128 * g, 64), :] = zero64
    S4F[...] = jnp.zeros_like(S4F)
    Q4F[...] = jnp.zeros_like(Q4F)
    QF[:, 384:416, :] = jnp.zeros((6, 32, 128), F32)

    for copy in c_tok:
        copy.wait()

    @pl.when(mine != 0)
    def _():
        pl.semaphore_wait(barrier, len(greeted))

    for peer, gap in greeted:
        @pl.when(gap == 0)
        def _():
            signal(lead_sem, peer)

    @pl.when(mine == 0)
    def _():
        pl.semaphore_wait(lead_sem, len(greeted))
        for d in range(1, 4):
            signal(barrier, far_lead(d))

    def remote(src, dst, ssem, rsem, peer):
        return pltpu.make_async_remote_copy(
            src_ref=src, dst_ref=dst, send_sem=ssem, recv_sem=rsem,
            device_id=peer, device_id_type=MESH,
        )

    def own_copy(buf, ssem, rsem, way, p):
        peer = inner if way == 0 else outer
        return remote(buf.at[z, p], buf.at[z, p], ssem.at[way, p], rsem.at[z, p], peer)

    def own_send(buf, ssem, rsem, p):
        own_copy(buf, ssem, rsem, 0, p).start()

        @pl.when(u == 1)
        def _():
            own_copy(buf, ssem, rsem, 1, p).start()

    def pass_copy(buf, fsem, rsem, k, p):
        c = order[k]
        peer = inner if k == 1 else outer
        return remote(buf.at[c, p], buf.at[c, p], fsem.at[k, p], rsem.at[c, p], peer)

    def line_sent(buf, ssem, fsem, rsem, pieces):
        for p in range(pieces):
            own_copy(buf, ssem, rsem, 0, p).wait_send()

        @pl.when(u == 1)
        def _():
            for p in range(pieces):
                own_copy(buf, ssem, rsem, 1, p).wait_send()
                for k in range(1, 4):
                    pass_copy(buf, fsem, rsem, k, p).wait_send()

    sent = []

    for p in range(2):
        own_send(X, tok_s, tok_r, p)

    c_gain.wait()
    for copy in c_qkv:
        copy.wait()
    gain_row = gain_v[...][None, :]
    o2 = [off[0, 3 * z + h] for h in range(3)]
    o3 = [off[1, 3 * z + h] for h in range(3)]
    o4 = [off[2, 3 * z + h] for h in range(3)]
    row16 = lax.broadcasted_iota(jnp.int32, (16, 128), 0)
    zero8 = jnp.zeros((8, 128), F32)

    def near_copy(c, d):
        peer = (s_base + quad_base + lax.rem(quad + d, 4), z)
        return remote(BX.at[yc, c], BX.at[yc, c], bx_s.at[d], bx_r.at[d], peer)

    def far_copy(c, j):
        peer = (s_base + far_base + lax.rem(quad + j, 4), z)
        piece = BX.at[yc, c, pl.ds(96, 48)]
        return remote(piece, piece, bx_s.at[4 + j], bx_r.at[4 + j], peer)

    for k in range(4):
        c = z if k == 0 else order[k]
        if k:
            for p in range(2):
                arriving = pass_copy(X, tok_f, tok_r, k, p)
                arriving.wait_recv()

                @pl.when(u == 1)
                def _():
                    arriving.start()

        normed = layer_norm(X[c].reshape(96, 768), gain_row)
        rows = pl.ds(pl.multiple_of(c * 96, 96), 96)
        every = nt_dot(normed, WQ[...]).astype(BF16)
        for t in range(6):
            part = every[:, 128 * t : 128 * t + 128]
            QB[t, rows, :] = part
            QF[t, rows, :] = part.astype(F32)
        for h in range(3):
            two = QF[3 + h, pl.ds(c * 96 + o2[h], 24, stride=4), :]
            BX[yc, c, 32 * h : 32 * h + 32, :] = jnp.concatenate([two, zero8], 0).astype(BF16)
            three = QF[3 + h, pl.ds(c * 96 + o3[h], 16, stride=8), :]
            BX[yc, c, 96 + 16 * h : 112 + 16 * h, :] = jnp.where(row16 < 12, three, 0.0).astype(BF16)
        for d in range(1, 4):
            near_copy(c, d).start()
        for j in range(4):
            far_copy(c, j).start()

    lane = lax.broadcasted_iota(jnp.int32, (1, 128), 1)
    left = lane < 64
    right = lane >= 64
    out_lanes = (left, right, right)

    for h in range(3):
        for j in range(3):
            S4F[3 * h + j : 3 * h + j + 1, :] = QF[3 + h, pl.ds(o4[h] + 128 * j, 1), :]
            Q4F[3 * h + j : 3 * h + j + 1, :] = QF[h, pl.ds(o4[h] + 128 * j, 1), :]
    G1[zx] = S4F[...].astype(BF16)

    @pl.when(mine == 0)
    def _():
        pl.semaphore_wait(barrier, 3)
        for d in range(1, 4):
            signal(go_sem, x_peer(d))
        for d in range(1, 8):
            signal(go_sem, yc_peer(d))

    def branch_one(h):
        kv = QB[3 + h]
        for i in range(3):
            rows = pl.ds(128 * i, 128)
            T1[h, rows, :] = attend(QB[h, rows, :], kv, out_lanes[h])

    branch_one(0)
    branch_one(1)

    @pl.when(mine != 0)
    def _():
        pl.semaphore_wait(go_sem, 1)

        @pl.when(yc == z)
        def _():
            for d in range(1, 8):
                signal(go_sem, yc_peer(d))

    g1_copies = [
        remote(G1.at[zx], G1.at[zx], g1_s.at[d], g1_r.at[d], zx_peer(d)) for d in range(1, 16)
    ]
    for copy in g1_copies:
        copy.start()
    sent += g1_copies

    branch_one(2)

    for d in range(1, 4):
        src = quad_base + lax.rem(quad - d + 4, 4)
        remote(BX.at[src], BX.at[src], bx_s.at[d], bx_r.at[d], inner).wait_recv()
    for j in range(4):
        src = far_base + lax.rem(quad - j + 4, 4)
        piece = BX.at[src, :, pl.ds(96, 48)]
        remote(piece, piece, bx_s.at[4 + j], bx_r.at[4 + j], inner).wait_recv()

    key = lax.broadcasted_iota(jnp.int32, (1, 512), 1)
    full2 = (key & 31) < 24
    full3 = (key & 15) < 12

    def branch_two(h):
        kv = jnp.concatenate(
            [BX[quad_base + m, c, 32 * h : 32 * h + 32, :] for m in range(4) for c in range(4)], axis=0
        )
        q = QF[h, pl.ds(o2[h], 96, stride=4), :].astype(BF16)
        tile = attend(q, kv, out_lanes[h], full2)
        for p in range(4):
            E2[h, pl.ds(p, 96, stride=4), :] = tile

    def branch_three(h):
        kv = jnp.concatenate(
            [BX[m, c, 96 + 16 * h : 112 + 16 * h, :] for m in range(8) for c in range(4)], axis=0
        )
        q = QF[h, pl.ds(o3[h], 48, stride=8), :].astype(BF16)
        tile = attend(q, kv, out_lanes[h], full3)
        for p in range(8):
            E3[h, pl.ds(p, 48, stride=8), :] = tile

    token = lax.broadcasted_iota(jnp.int32, (384, 128), 0)

    def merge(h):
        t1, t2, t3 = T1[h], E2[h], E3[h]
        l1, l2, l3 = (pltpu.roll(t, 64, 1) for t in (t1, t2, t3))
        c2 = (token & 3) == o2[h]
        c3 = (token & 7) == o3[h]
        peak = jnp.where(c2, jnp.maximum(l1, l2), l1)
        peak = jnp.where(c3, jnp.maximum(peak, l3), peak)
        w1 = jnp.exp2(l1 - peak)
        w2 = jnp.where(c2, jnp.exp2(l2 - peak), 0.0)
        w3 = jnp.where(c3, jnp.exp2(l3 - peak), 0.0)
        den = w1 + w2 + w3
        out = (w1 * t1 + w2 * t2 + w3 * t3) / den
        lse = peak + jnp.log(den) * LOG2E
        MR[h] = jnp.where(out_lanes[h], out, pltpu.roll(lse, 64, 1))
        return out

    for h in range(2):
        branch_two(h)
        branch_three(h)
    m01 = jnp.where(left, merge(0), merge(1)).astype(BF16)
    for p in range(2):
        AA[z, p] = m01[192 * p : 192 * p + 192]
        own_send(AA, aa_s, aa_r, p)
    branch_two(2)
    branch_three(2)
    m2 = merge(2)
    AA[z, 2] = jnp.where(left, pltpu.roll(m2[:192], 64, 1), m2[192:]).astype(BF16)
    own_send(AA, aa_s, aa_r, 2)

    @pl.when(u == 1)
    def _():
        for k, p in [(2, p) for p in range(3)]:
            arriving = pass_copy(AA, aa_f, aa_r, k, p)
            arriving.wait_recv()
            arriving.start()

    for d in range(1, 16):
        src = lax.rem(zx - d + 16, 16)
        remote(G1.at[src], G1.at[src], g1_s.at[d], g1_r.at[d], zx_peer(d)).wait_recv()
    row_to = lax.broadcasted_iota(jnp.int32, (144, 256), 0)
    row_from = lax.broadcasted_iota(jnp.int32, (144, 256), 1)
    ninth = (row_to * 7282) >> 16
    pick = (row_from == row_to + 7 * ninth).astype(F32).astype(BF16)
    G2[yc] = jnp.dot(pick, G1[...].reshape(256, 128), preferred_element_type=F32).astype(BF16)
    g2_copies = [
        remote(G2.at[yc], G2.at[yc], g2_s.at[d], g2_r.at[d], yc_peer(d)) for d in range(1, 8)
    ]
    for copy in g2_copies:
        copy.start()
    sent += g2_copies

    @pl.when(u == 1)
    def _():
        for k, p in [(k, p) for p in range(3) for k in (1, 3)]:
            arriving = pass_copy(AA, aa_f, aa_r, k, p)
            arriving.wait_recv()
            arriving.start()

    for d in range(1, 8):
        src = lax.rem(yc - d + 8, 8)
        remote(G2.at[src], G2.at[src], g2_s.at[d], g2_r.at[d], yc_peer(d)).wait_recv()
    kv4 = G2[...].reshape(1152, 128)
    key4 = lax.broadcasted_iota(jnp.int32, (1, 1152), 1)
    key_at = key4 - 9 * ((key4 * 7282) >> 16)
    query4 = lax.broadcasted_iota(jnp.int32, (16, 1), 0)

    def head_row(r):
        return jnp.where(r < 3, 0, jnp.where(r < 6, 1, jnp.where(r < 9, 2, 3)))

    keep = head_row(key_at) == head_row(query4)
    lane16 = lax.broadcasted_iota(jnp.int32, (16, 128), 1)
    out16 = (row16 < 3) == (lane16 < 64)
    tile4 = attend(Q4F[...].astype(BF16), kv4, out16, keep)
    for h in range(3):
        for j in range(3):
            S4F[3 * h + j : 3 * h + j + 1, :] = MR[h, pl.ds(o4[h] + 128 * j, 1), :]
    tile1 = S4F[...]
    l1 = pltpu.roll(tile1, 64, 1)
    l4 = pltpu.roll(tile4, 64, 1)
    peak = jnp.maximum(l1, l4)
    w1 = jnp.exp2(l1 - peak)
    w4 = jnp.exp2(l4 - peak)
    both = (w1 * tile1 + w4 * tile4) / (w1 + w4)
    turned = pltpu.roll(both, 64, 1)
    PF[...] = jnp.zeros_like(PF)
    PF[0:3, :] = jnp.where(left, both[0:3], both[3:6])
    PF[3:6, :] = jnp.where(left, turned[6:9], both[6:9])
    PT[z] = PF[...].astype(BF16)
    pt_copies = [
        remote(PT.at[z], PT.at[z], pt_s.at[d], pt_r.at[d], head_peer(d)) for d in range(1, 4)
    ]
    for copy in pt_copies:
        copy.start()
    sent += pt_copies

    for copy in c_late:
        copy.wait()

    @pl.when(u == 0)
    def _():
        for k in range(1, 4):
            for p in range(3):
                pass_copy(AA, aa_f, aa_r, k, p).wait_recv()

    for d in range(1, 4):
        src = lax.rem(z - d + 4, 4)
        remote(PT.at[src], PT.at[src], pt_s.at[d], pt_r.at[d], head_peer(d)).wait_recv()
    tok192 = lax.broadcasted_iota(jnp.int32, (192, 128), 0)
    tok_packed = tok192 + jnp.where(left, 0, 192)
    pieces = []
    for g in range(4):
        patch = PT[g].astype(F32)
        o01 = jnp.where(left, off[2, 3 * g], off[2, 3 * g + 1])
        places = (
            (tok192, o01, 0, (0, 1)), (tok192 + 192, o01, 0, (1, 2)),
            (tok_packed, off[2, 3 * g + 2], 3, (0, 1, 2)),
        )
        fixed = []
        for p, (at, offset, first, groups) in enumerate(places):
            piece = AA[g, p].astype(F32)
            for j in groups:
                piece = jnp.where(at == offset + 128 * j, patch[first + j : first + j + 1], piece)
            fixed.append(piece.astype(BF16))
        pieces.append(fixed)
    for half in range(2):
        first = jnp.concatenate([pieces[g][half] for g in range(4)], axis=1)
        second = jnp.concatenate([pieces[g][2] for g in range(4)], axis=1)
        acc = jnp.dot(first, W01[...], preferred_element_type=F32)
        acc = acc + jnp.dot(second, W2[half], preferred_element_type=F32)
        own = X[2 * half : 2 * half + 2].reshape(192, 768).astype(F32)
        L[192 * half : 192 * half + 192, :] = (own + acc).astype(BF16)
    c_layer = pltpu.make_async_copy(
        L.at[pl.ds(pl.multiple_of(z * 96, 96), 96)], layer_out, out_sem.at[0]
    )
    c_layer.start()

    col = lax.broadcasted_iota(jnp.int32, (64, 384), 1)

    def part(dy):
        p = nt_dot(WD[192 * dy : 192 * dy + 192, :], L[...])
        before = jnp.where(col == 0, 0.0, pltpu.roll(p[0:64], 1, 1))
        after = jnp.where(col == 383, 0.0, pltpu.roll(p[128:192], 383, 1))
        return before + p[64:128] + after

    HS[0] = part(0).astype(BF16)
    h_up = remote(HS.at[0], HR.at[0], h_s.at[0], h_r.at[0], up)
    h_up.start()
    HS[1] = part(2).astype(BF16)
    h_down = remote(HS.at[1], HR.at[1], h_s.at[1], h_r.at[1], down)
    h_down.start()
    middle = part(1)
    line_sent(X, tok_s, tok_f, tok_r, 2)
    line_sent(AA, aa_s, aa_f, aa_r, 3)
    for d in range(1, 4):
        remote(BX.at[yc], BX.at[yc], bx_s.at[d], bx_r.at[d], inner).wait_send()
    for j in range(4):
        piece = BX.at[yc, :, pl.ds(96, 48)]
        remote(piece, piece, bx_s.at[4 + j], bx_r.at[4 + j], inner).wait_send()
    for copy in sent:
        copy.wait_send()
    h_up.wait_recv()
    h_down.wait_recv()
    conv = middle + jnp.where(s > 0, HR[0].astype(F32), 0.0)
    conv = conv + jnp.where(s < 127, HR[1].astype(F32), 0.0)
    DO[...] = (0.5 * conv * (1.0 + lax.erf(conv * 0.7071067811865476))).astype(BF16)
    c_dec = pltpu.make_async_copy(DO, dec_out, out_sem.at[1])
    c_dec.start()
    h_up.wait_send()
    h_down.wait_send()
    c_layer.wait()
    c_dec.wait()


def shards(tokens, norm_gain, qkv_weight, out_weight, dec_weight, offsets):
    wqkv = qkv_weight.reshape(576, 768)
    wdec = jnp.transpose(dec_weight, (1, 2, 0, 3)).reshape(576, 768)
    vm = pltpu.VMEM
    dma = pltpu.SemaphoreType.DMA
    layer, decoded = pl.pallas_call(
        body,
        out_shape=(
            jax.ShapeDtypeStruct((96, 768), BF16),
            jax.ShapeDtypeStruct((64, 384), BF16),
        ),
        in_specs=[pl.BlockSpec(memory_space=pl.ANY)] * 5
        + [pl.BlockSpec(memory_space=pltpu.SMEM)],
        out_specs=(pl.BlockSpec(memory_space=pl.ANY),) * 2,
        scratch_shapes=[
            vm((4, 2, 48, 768), BF16),
            vm((768,), F32),
            vm((768, 768), BF16),
            vm((512, 768), BF16),
            vm((2, 512, 768), BF16),
            vm((576, 768), BF16),
            vm((6, 384, 128), BF16),
            vm((6, 416, 128), F32),
            vm((8, 4, 144, 128), BF16),
            vm((16, 128), F32),
            vm((16, 128), F32),
            vm((16, 16, 128), BF16),
            vm((8, 144, 128), BF16),
            vm((3, 384, 128), F32),
            vm((3, 384, 128), F32),
            vm((3, 384, 128), F32),
            vm((3, 384, 128), F32),
            vm((4, 3, 192, 128), BF16),
            vm((16, 128), F32),
            vm((4, 16, 128), BF16),
            vm((384, 768), BF16),
            vm((2, 64, 384), BF16),
            vm((2, 64, 384), BF16),
            vm((64, 384), BF16),
            dma((26,)),
            dma((2, 2)), dma((4, 2)), dma((4, 2)),
            dma((8,)), dma((8,)),
            dma((16,)), dma((16,)),
            dma((8,)), dma((8,)),
            dma((2, 3)), dma((4, 3)), dma((4, 3)),
            dma((4,)), dma((4,)),
            dma((2,)), dma((2,)),
            dma((2,)),
            pltpu.SemaphoreType.REGULAR, pltpu.SemaphoreType.REGULAR,
        ],
        compiler_params=pltpu.CompilerParams(
            collective_id=0, has_side_effects=True, vmem_limit_bytes=60 * 1024 * 1024
        ),
        cost_estimate=pl.CostEstimate(
            flops=1500000000, bytes_accessed=4000000, transcendentals=700000
        ),
        name="dilated_layer",
    )(tokens, norm_gain, wqkv, out_weight, wdec, offsets)
    return layer, decoded.reshape(64, 1, 384)


def solution(mesh):
    placed = (
        P(("seq", "head"), None),
        P(),
        P(None, "head", None, None),
        P(),
        P("head", None, None, None),
        P(),
    )
    return jax.shard_map(
        shards,
        mesh=mesh,
        in_specs=placed,
        out_specs=(P(("seq", "head"), None), P("head", "seq", None)),
        check_vma=False,
    )
```

time: 73.2 us -> 61.9 us (0.85)
  the two profiles are of different devices: /device:TPU:95 before, /device:TPU:31 now
where the time goes in v2:
time: 61.9 us; the launch traced here: 61.7 us
  Pallas kernels  58.1 us (94%)
  local copies, waits for them, and re-layouts  3 us (5%)
  between operations  0.64 us (1%)
    pallas_call x1, Pallas kernels, shards(): pl.pallas_call(body, out_shape=(jax.ShapeDtypeStruct((96, 768), BF16), ja...  58.1 us
    unnamed x2, local copies, waits for them, and re-layouts  3 us

profile of v2, /device:TPU:31, one launch (start us, length us, event | category | flops | bytes accessed | tf_op | source)
XLA Modules:
  0.0 61.7 jit_solution(9369611887310238661)
XLA Ops:
  0.6 58.1 %dilated_layer.1 = (bf16[96,768]{1,0:T(8,128)(2,1)}, bf16[64,384]{1,0:T(8,128)(2,1)}) custom-call(bf16[96,768]{1,0:T(8,128)(2,1)} %tok.1, f32[768]{0:T(1024)} %gain.1, bf16[576,768]{1,0:T(8,128)(2,1)} %bitcast.6, bf16[768,768]{1,0:T(8,128)(2,1)} %wout.1, bf16[576,768]{1,0:T(8,128)(2,1)} %bitcast.7, s32[3,12]{1,0:T(4,128)} %off.1), custom_call_target="tpu_custom_call" | custom-call | flops 1500000000 | bytes 4000000 | tf_op jit(solution)/shard_map/dilated_layer/pallas_call | solution.py:495
  58.7 1.6 %copy.10 = bf16[96,768]{1,0:T(8,128)(2,1)} copy(bf16[96,768]{1,0:T(8,128)(2,1)} %get-tuple-element.8) | data formatting | bytes 294912
  60.3 1.4 %copy.11 = bf16[64,1,384]{2,0,1:T(8,128)(2,1)} copy(bf16[64,1,384]{2,0,1:T(8,128)(2,1)} %bitcast.5) | data formatting | bytes 98304

commit v3 on v2

--- a/solution.py
+++ b/solution.py
@@ -46,9 +46,9 @@
     layer_out, dec_out,
     X, gain_v, WQ, W01, W2, WD, QB, QF,
     BX, S4F, Q4F, G1, G2,
-    T1, E2, E3, MR, AA, PF, PT, L, HS, HR, DO,
+    T1, E2, E3, MR, AA, PF, PT, L, HS, HR,
     in_sem, tok_s, tok_f, tok_r, bx_s, bx_r, g1_s, g1_r, g2_s, g2_r,
-    aa_s, aa_f, aa_r, pt_s, pt_r, h_s, h_r, out_sem, lead_sem, go_sem,
+    aa_s, aa_f, aa_r, pt_s, pt_r, h_s, h_r, lead_sem, go_sem,
 ):
     s = lax.axis_index("seq")
     z = lax.axis_index("head")
@@ -210,6 +210,16 @@
 
     for k in range(4):
         c = z if k == 0 else order[k]
+        if k == 3:
+
+            @pl.when(mine == 0)
+            def _():
+                pl.semaphore_wait(barrier, 3)
+                for d in range(1, 4):
+                    signal(go_sem, x_peer(d))
+                for d in range(1, 8):
+                    signal(go_sem, yc_peer(d))
+
         if k:
             for p in range(2):
                 arriving = pass_copy(X, tok_f, tok_r, k, p)
@@ -247,31 +257,26 @@
             Q4F[3 * h + j : 3 * h + j + 1, :] = QF[h, pl.ds(o4[h] + 128 * j, 1), :]
     G1[zx] = S4F[...].astype(BF16)
 
-    @pl.when(mine == 0)
-    def _():
-        pl.semaphore_wait(barrier, 3)
-        for d in range(1, 4):
-            signal(go_sem, x_peer(d))
-        for d in range(1, 8):
-            signal(go_sem, yc_peer(d))
-
     def branch_one(h):
         kv = QB[3 + h]
         for i in range(3):
             rows = pl.ds(128 * i, 128)
             T1[h, rows, :] = attend(QB[h, rows, :], kv, out_lanes[h])
 
+    @pl.when(yc == z)
+    def _():
+        @pl.when(x != z)
+        def _():
+            pl.semaphore_wait(go_sem, 1)
+            for d in range(1, 8):
+                signal(go_sem, yc_peer(d))
+
     branch_one(0)
     branch_one(1)
 
-    @pl.when(mine != 0)
+    @pl.when(yc != z)
     def _():
         pl.semaphore_wait(go_sem, 1)
-
-        @pl.when(yc == z)
-        def _():
-            for d in range(1, 8):
-                signal(go_sem, yc_peer(d))
 
     g1_copies = [
         remote(G1.at[zx], G1.at[zx], g1_s.at[d], g1_r.at[d], zx_peer(d)) for d in range(1, 16)
@@ -337,6 +342,7 @@
     for p in range(2):
         AA[z, p] = m01[192 * p : 192 * p + 192]
         own_send(AA, aa_s, aa_r, p)
+
     branch_two(2)
     branch_three(2)
     m2 = merge(2)
@@ -445,10 +451,6 @@
         acc = acc + jnp.dot(second, W2[half], preferred_element_type=F32)
         own = X[2 * half : 2 * half + 2].reshape(192, 768).astype(F32)
         L[192 * half : 192 * half + 192, :] = (own + acc).astype(BF16)
-    c_layer = pltpu.make_async_copy(
-        L.at[pl.ds(pl.multiple_of(z * 96, 96), 96)], layer_out, out_sem.at[0]
-    )
-    c_layer.start()
 
     col = lax.broadcasted_iota(jnp.int32, (64, 384), 1)
 
@@ -460,10 +462,19 @@
 
     HS[0] = part(0).astype(BF16)
     h_up = remote(HS.at[0], HR.at[0], h_s.at[0], h_r.at[0], up)
-    h_up.start()
+
+    @pl.when(s < 127)
+    def _():
+        h_up.start()
+
     HS[1] = part(2).astype(BF16)
     h_down = remote(HS.at[1], HR.at[1], h_s.at[1], h_r.at[1], down)
-    h_down.start()
+
+    @pl.when(s > 0)
+    def _():
+        h_down.start()
+
+    layer_out[...] = L[pl.ds(pl.multiple_of(z * 96, 96), 96), :]
     middle = part(1)
     line_sent(X, tok_s, tok_f, tok_r, 2)
     line_sent(AA, aa_s, aa_f, aa_r, 3)
@@ -474,17 +485,20 @@
         remote(piece, piece, bx_s.at[4 + j], bx_r.at[4 + j], inner).wait_send()
     for copy in sent:
         copy.wait_send()
-    h_up.wait_recv()
-    h_down.wait_recv()
+
+    @pl.when(s > 0)
+    def _():
+        h_up.wait_recv()
+        h_down.wait_send()
+
+    @pl.when(s < 127)
+    def _():
+        h_down.wait_recv()
+        h_up.wait_send()
+
     conv = middle + jnp.where(s > 0, HR[0].astype(F32), 0.0)
     conv = conv + jnp.where(s < 127, HR[1].astype(F32), 0.0)
-    DO[...] = (0.5 * conv * (1.0 + lax.erf(conv * 0.7071067811865476))).astype(BF16)
-    c_dec = pltpu.make_async_copy(DO, dec_out, out_sem.at[1])
-    c_dec.start()
-    h_up.wait_send()
-    h_down.wait_send()
-    c_layer.wait()
-    c_dec.wait()
+    dec_out[...] = (0.5 * conv * (1.0 + lax.erf(conv * 0.7071067811865476))).astype(BF16)
 
 
 def shards(tokens, norm_gain, qkv_weight, out_weight, dec_weight, offsets):
@@ -495,12 +509,12 @@
     layer, decoded = pl.pallas_call(
         body,
         out_shape=(
-            jax.ShapeDtypeStruct((96, 768), BF16),
-            jax.ShapeDtypeStruct((64, 384), BF16),
+            pltpu.VMEM((96, 768), BF16),
+            pltpu.VMEM((64, 384), BF16),
         ),
         in_specs=[pl.BlockSpec(memory_space=pl.ANY)] * 5
         + [pl.BlockSpec(memory_space=pltpu.SMEM)],
-        out_specs=(pl.BlockSpec(memory_space=pl.ANY),) * 2,
+        out_specs=(pl.BlockSpec(memory_space=pltpu.VMEM),) * 2,
         scratch_shapes=[
             vm((4, 2, 48, 768), BF16),
             vm((768,), F32),
@@ -525,7 +539,6 @@
             vm((384, 768), BF16),
             vm((2, 64, 384), BF16),
             vm((2, 64, 384), BF16),
-            vm((64, 384), BF16),
             dma((26,)),
             dma((2, 2)), dma((4, 2)), dma((4, 2)),
             dma((8,)), dma((8,)),
@@ -534,7 +547,6 @@
             dma((2, 3)), dma((4, 3)), dma((4, 3)),
             dma((4,)), dma((4,)),
             dma((2,)), dma((2,)),
-            dma((2,)),
             pltpu.SemaphoreType.REGULAR, pltpu.SemaphoreType.REGULAR,
         ],
         compiler_params=pltpu.CompilerParams(

time: 61.9 us -> 58.9 us (0.952)
  local copies, waits for them, and re-layouts: 3 us -> 1.28 us
  Pallas kernels: 58.1 us -> 56.9 us
    unnamed x2, local copies, waits for them, and re-layouts: 3 us -> 1.28 us
    pallas_call x1, Pallas kernels: 58.1 us -> 56.9 us  [shards(): pl.pallas_call(body, out_shape=(pltpu.VMEM((96, 768), BF16), pltpu.VMEM((...]
where the time goes in v3:
time: 58.9 us; the launch traced here: 58.8 us
  Pallas kernels  56.9 us (97%)
  local copies, waits for them, and re-layouts  1.28 us (2%)
  between operations  0.64 us (1%)
    pallas_call x1, Pallas kernels, shards(): pl.pallas_call(body, out_shape=(pltpu.VMEM((96, 768), BF16), pltpu.VMEM((...  56.9 us
    unnamed x2, local copies, waits for them, and re-layouts  1.28 us

profile of v3, /device:TPU:31, one launch (start us, length us, event | category | flops | bytes accessed | tf_op | source)
XLA Modules:
  0.0 58.8 jit_solution(17694914296615319825)
XLA Ops:
  0.6 56.9 %dilated_layer.1 = (bf16[96,768]{1,0:T(8,128)(2,1)S(1)}, bf16[64,384]{1,0:T(8,128)(2,1)S(1)}) custom-call(bf16[96,768]{1,0:T(8,128)(2,1)} %tok.1, f32[768]{0:T(1024)} %gain.1, bf16[576,768]{1,0:T(8,128)(2,1)} %bitcast.6, bf16[768,768]{1,0:T(8,128)(2,1)} %wout.1, bf16[576,768]{1,0:T(8,128)(2,1)} %bitcast.7, s32[3,12]{1,0:T(4,128)} %off.1), custom_call_target="tpu_custom_call" | custom-call | flops 1500000000 | bytes 4000000 | tf_op jit(solution)/shard_map/dilated_layer/pallas_call | solution.py:509
  57.5 0.7 %copy.10 = bf16[96,768]{1,0:T(8,128)(2,1)} copy(bf16[96,768]{1,0:T(8,128)(2,1)S(1)} %get-tuple-element.6) | data formatting | bytes 294912
  58.2 0.6 %copy.11 = bf16[64,1,384]{2,0,1:T(8,128)(2,1)} copy(bf16[64,1,384]{2,0,1:T(8,128)(2,1)S(1)} %bitcast.5) | data formatting | bytes 98304

commit v4 on v3

--- a/solution.py
+++ b/solution.py
@@ -79,13 +79,14 @@
     down = (lax.rem(s + 127, 128), z)
 
     x = lax.rem(zx, 4)
+    zh = lax.div(zx, 4)
     barrier = pltpu.get_barrier_semaphore()
 
     def signal(sem, peer):
         pl.semaphore_signal(sem, inc=1, device_id=peer, device_id_type=MESH)
 
     def from_lead(x_at, yc_at, z_at):
-        return (x_at - z_at) * (x_at - z_at) + (yc_at - z_at) * (yc_at - z_at)
+        return (x_at - z_at) * (x_at - z_at) + (yc_at - z_at - 2) * (yc_at - z_at - 2)
 
     def x_peer(d):
         return ((zx - x + lax.rem(x + d, 4)) * 8 + yc, z)
@@ -208,17 +209,31 @@
         piece = BX.at[yc, c, pl.ds(96, 48)]
         return remote(piece, piece, bx_s.at[4 + j], bx_r.at[4 + j], peer)
 
+    def lead_word():
+        @pl.when(mine == 0)
+        def _():
+            pl.semaphore_wait(barrier, 3)
+            for d in range(1, 4):
+                signal(go_sem, x_peer(d))
+            for d in range(1, 8):
+                signal(go_sem, yc_peer(d))
+
+    def head_word():
+        @pl.when(yc == z + 2)
+        def _():
+            @pl.when(x != z)
+            def _():
+                pl.semaphore_wait(go_sem, 1)
+                for d in range(1, 8):
+                    signal(go_sem, yc_peer(d))
+
     for k in range(4):
         c = z if k == 0 else order[k]
         if k == 3:
 
-            @pl.when(mine == 0)
+            @pl.when(zh != 0)
             def _():
-                pl.semaphore_wait(barrier, 3)
-                for d in range(1, 4):
-                    signal(go_sem, x_peer(d))
-                for d in range(1, 8):
-                    signal(go_sem, yc_peer(d))
+                lead_word()
 
         if k:
             for p in range(2):
@@ -263,29 +278,40 @@
             rows = pl.ds(128 * i, 128)
             T1[h, rows, :] = attend(QB[h, rows, :], kv, out_lanes[h])
 
-    @pl.when(yc == z)
-    def _():
-        @pl.when(x != z)
-        def _():
-            pl.semaphore_wait(go_sem, 1)
-            for d in range(1, 8):
-                signal(go_sem, yc_peer(d))
-
-    branch_one(0)
-    branch_one(1)
-
-    @pl.when(yc != z)
-    def _():
-        pl.semaphore_wait(go_sem, 1)
-
     g1_copies = [
         remote(G1.at[zx], G1.at[zx], g1_s.at[d], g1_r.at[d], zx_peer(d)) for d in range(1, 16)
     ]
-    for copy in g1_copies:
-        copy.start()
     sent += g1_copies
 
+    def row_word():
+        @pl.when(yc != z + 2)
+        def _():
+            pl.semaphore_wait(go_sem, 1)
+
+        for copy in g1_copies:
+            copy.start()
+
+    @pl.when(zh != 0)
+    def _():
+        head_word()
+
+    @pl.when(zh == 0)
+    def _():
+        lead_word()
+
+    branch_one(0)
+    branch_one(1)
+
+    @pl.when(zh == 0)
+    def _():
+        head_word()
+
+    @pl.when(zh != 0)
+    def _():
+        row_word()
+
     branch_one(2)
+
 
     for d in range(1, 4):
         src = quad_base + lax.rem(quad - d + 4, 4)
@@ -335,6 +361,10 @@
         MR[h] = jnp.where(out_lanes[h], out, pltpu.roll(lse, 64, 1))
         return out
 
+    @pl.when(zh == 0)
+    def _():
+        row_word()
+
     for h in range(2):
         branch_two(h)
         branch_three(h)
@@ -351,7 +381,7 @@
 
     @pl.when(u == 1)
     def _():
-        for k, p in [(2, p) for p in range(3)]:
+        for k, p in ((2, 0), (2, 1)):
             arriving = pass_copy(AA, aa_f, aa_r, k, p)
             arriving.wait_recv()
             arriving.start()
@@ -373,7 +403,7 @@
 
     @pl.when(u == 1)
     def _():
-        for k, p in [(k, p) for p in range(3) for k in (1, 3)]:
+        for k, p in ((2, 2), (1, 0), (3, 0), (1, 1), (3, 1), (1, 2), (3, 2)):
             arriving = pass_copy(AA, aa_f, aa_r, k, p)
             arriving.wait_recv()
             arriving.start()
@@ -460,19 +490,19 @@
         after = jnp.where(col == 383, 0.0, pltpu.roll(p[128:192], 383, 1))
         return before + p[64:128] + after
 
+    HS[1] = part(2).astype(BF16)
+    h_down = remote(HS.at[1], HR.at[1], h_s.at[1], h_r.at[1], down)
+
+    @pl.when(s > 0)
+    def _():
+        h_down.start()
+
     HS[0] = part(0).astype(BF16)
     h_up = remote(HS.at[0], HR.at[0], h_s.at[0], h_r.at[0], up)
 
     @pl.when(s < 127)
     def _():
         h_up.start()
-
-    HS[1] = part(2).astype(BF16)
-    h_down = remote(HS.at[1], HR.at[1], h_s.at[1], h_r.at[1], down)
-
-    @pl.when(s > 0)
-    def _():
-        h_down.start()
 
     layer_out[...] = L[pl.ds(pl.multiple_of(z * 96, 96), 96), :]
     middle = part(1)

time: 58.9 us -> 58.4 us (level)
  Pallas kernels: 56.9 us -> 56.3 us
where the time goes in v4:
time: 58.4 us; the launch traced here: 58.3 us
  Pallas kernels  56.3 us (96%)
  local copies, waits for them, and re-layouts  1.28 us (2%)
  between operations  0.64 us (1%)
    pallas_call x1, Pallas kernels, shards(): pl.pallas_call(body, out_shape=(pltpu.VMEM((96, 768), BF16), pltpu.VMEM((...  56.3 us
    unnamed x2, local copies, waits for them, and re-layouts  1.28 us

profile of v4, /device:TPU:31, one launch (start us, length us, event | category | flops | bytes accessed | tf_op | source)
XLA Modules:
  0.0 58.3 jit_solution(3827088661230050748)
XLA Ops:
  0.6 56.3 %dilated_layer.1 = (bf16[96,768]{1,0:T(8,128)(2,1)S(1)}, bf16[64,384]{1,0:T(8,128)(2,1)S(1)}) custom-call(bf16[96,768]{1,0:T(8,128)(2,1)} %tok.1, f32[768]{0:T(1024)} %gain.1, bf16[576,768]{1,0:T(8,128)(2,1)} %bitcast.6, bf16[768,768]{1,0:T(8,128)(2,1)} %wout.1, bf16[576,768]{1,0:T(8,128)(2,1)} %bitcast.7, s32[3,12]{1,0:T(4,128)} %off.1), custom_call_target="tpu_custom_call" | custom-call | flops 1500000000 | bytes 4000000 | tf_op jit(solution)/shard_map/dilated_layer/pallas_call | solution.py:539
  57.0 0.7 %copy.10 = bf16[96,768]{1,0:T(8,128)(2,1)} copy(bf16[96,768]{1,0:T(8,128)(2,1)S(1)} %get-tuple-element.6) | data formatting | bytes 294912
  57.6 0.6 %copy.11 = bf16[64,1,384]{2,0,1:T(8,128)(2,1)} copy(bf16[64,1,384]{2,0,1:T(8,128)(2,1)S(1)} %bitcast.5) | data formatting | bytes 98304

commit v5 on v4

--- a/solution.py
+++ b/solution.py
@@ -132,7 +132,7 @@
         W2[1, pl.ds(128 * g, 64), :] = zero64
     S4F[...] = jnp.zeros_like(S4F)
     Q4F[...] = jnp.zeros_like(Q4F)
-    QF[:, 384:416, :] = jnp.zeros((6, 32, 128), F32)
+    QF[:, 384:424, :] = jnp.zeros((6, 40, 128), F32)
 
     for copy in c_tok:
         copy.wait()
@@ -346,7 +346,7 @@
     token = lax.broadcasted_iota(jnp.int32, (384, 128), 0)
 
     def merge(h):
-        t1, t2, t3 = T1[h], E2[h], E3[h]
+        t1, t2, t3 = T1[h], E2[h, 0:384, :], E3[h, 0:384, :]
         l1, l2, l3 = (pltpu.roll(t, 64, 1) for t in (t1, t2, t3))
         c2 = (token & 3) == o2[h]
         c3 = (token & 7) == o3[h]
@@ -553,15 +553,15 @@
             vm((2, 512, 768), BF16),
             vm((576, 768), BF16),
             vm((6, 384, 128), BF16),
-            vm((6, 416, 128), F32),
+            vm((6, 424, 128), F32),
             vm((8, 4, 144, 128), BF16),
             vm((16, 128), F32),
             vm((16, 128), F32),
             vm((16, 16, 128), BF16),
             vm((8, 144, 128), BF16),
             vm((3, 384, 128), F32),
-            vm((3, 384, 128), F32),
-            vm((3, 384, 128), F32),
+            vm((3, 392, 128), F32),
+            vm((3, 392, 128), F32),
             vm((3, 384, 128), F32),
             vm((4, 3, 192, 128), BF16),
             vm((16, 128), F32),

time: 58.4 us -> 58.4 us (level)
  no operation moved by 1% of the time
where the time goes in v5:
time: 58.4 us; the launch traced here: 58.3 us
  Pallas kernels  56.3 us (96%)
  local copies, waits for them, and re-layouts  1.28 us (2%)
  between operations  0.64 us (1%)
    pallas_call x1, Pallas kernels, shards(): pl.pallas_call(body, out_shape=(pltpu.VMEM((96, 768), BF16), pltpu.VMEM((...  56.3 us
    unnamed x2, local copies, waits for them, and re-layouts  1.28 us

profile of v5, /device:TPU:31, one launch (start us, length us, event | category | flops | bytes accessed | tf_op | source)
XLA Modules:
  0.0 58.3 jit_solution(13299810322809803560)
XLA Ops:
  0.6 56.3 %dilated_layer.1 = (bf16[96,768]{1,0:T(8,128)(2,1)S(1)}, bf16[64,384]{1,0:T(8,128)(2,1)S(1)}) custom-call(bf16[96,768]{1,0:T(8,128)(2,1)} %tok.1, f32[768]{0:T(1024)} %gain.1, bf16[576,768]{1,0:T(8,128)(2,1)} %bitcast.6, bf16[768,768]{1,0:T(8,128)(2,1)} %wout.1, bf16[576,768]{1,0:T(8,128)(2,1)} %bitcast.7, s32[3,12]{1,0:T(4,128)} %off.1), custom_call_target="tpu_custom_call" | custom-call | flops 1500000000 | bytes 4000000 | tf_op jit(solution)/shard_map/dilated_layer/pallas_call | solution.py:539
  57.0 0.7 %copy.10 = bf16[96,768]{1,0:T(8,128)(2,1)} copy(bf16[96,768]{1,0:T(8,128)(2,1)S(1)} %get-tuple-element.6) | data formatting | bytes 294912
  57.6 0.6 %copy.11 = bf16[64,1,384]{2,0,1:T(8,128)(2,1)} copy(bf16[64,1,384]{2,0,1:T(8,128)(2,1)S(1)} %bitcast.5) | data formatting | bytes 98304
